TPU v7x, 32 devices: a whole 2x2x4 slice. The times are simulated.
32 devices in a mesh: mesh: 4 (over y, core), mode: 8 (over z, x).
Axes of the slice: x: 2, y: 2, z: 4, core: 2. Of those that a mesh axis runs over, the one named last changes fastest.
Arguments:
- field: float32 [256, 512, 1024], P('mode', 'mesh'), may hold values from -6 to 6
- kappa: bfloat16 [3, 512, 1024], P(None, ('mesh', 'mode')), may hold values from 0.099609375 to 1
- mass: float32 [512, 1024], P(('mesh', 'mode')), may hold values from 0.5 to 1.5
- kl_modes: bfloat16 [3, 256, 256], replicated, may hold values from -0.375 to 0.375
- to_points: bfloat16 [512, 256], replicated, may hold values from -0.375 to 0.375
- from_points: bfloat16 [256, 512], replicated, may hold values from -0.25 to 0.25
- capacity: float32 [512], replicated, may hold values from 0.5 to 2
- latent: float32 [512], replicated, may hold values from 0.5 to 3
Outputs:
- residual: bfloat16 [256, 512, 1024], P('mode', 'mesh')
All inputs are finite; a program needn't handle non-finite values.
Results may differ from a plain program's by a relative error of at most 0.0058.
Values may be sent and summed in bfloat16 or wider, within the bound.
A program may use at most 256 MiB of HBM per device.

v0:
```python
import jax
import jax.numpy as jnp
from jax import lax
from jax.sharding import PartitionSpec as P


def extended(cells, sides, width):
    for axis, dim in sides:
        count = lax.axis_size(axis)
        ends = count - 1
        head = lax.slice_in_dim(cells, 0, width, axis=dim)
        tail = lax.slice_in_dim(cells, cells.shape[dim] - width, cells.shape[dim], axis=dim)
        cells = jnp.concatenate(
            [
                lax.ppermute(tail, axis, [(i, (i + 1) % count) for i in range(ends)]),
                cells,
                lax.ppermute(head, axis, [((i + 1) % count, i) for i in range(ends)]),
            ],
            axis=dim,
        )
    return cells


def conduct(values, kappa):
    count = values.shape[1] - 2
    width = values.shape[2]
    vals = jnp.pad(values.astype(jnp.float32), ((0, 0), (0, 0), (1, 1)))[None]
    kaps = jnp.pad(kappa.astype(jnp.float32), ((0, 0), (0, 0), (1, 1)))[:, None]
    centre = vals[:, :, 1 : 1 + count, 1 : 1 + width]
    kcentre = kaps[:, :, 1 : 1 + count, 1 : 1 + width]
    total = jnp.zeros((kaps.shape[0], vals.shape[1], count, width), jnp.float32)
    for shift_x, shift_y in ((0, 1), (2, 1), (1, 0), (1, 2)):
        other = vals[:, :, shift_x : shift_x + count, shift_y : shift_y + width]
        kother = kaps[:, :, shift_x : shift_x + count, shift_y : shift_y + width]
        total = total + 0.5 * (kcentre + kother) * (centre - other)
    return total.astype(jnp.bfloat16)


def finish(coarse, images, mass_rows, kl_modes, to_points, from_points, capacity, latent):
    mixed = jnp.einsum("kij,kjxy->ixy", kl_modes, images, preferred_element_type=jnp.float32)
    temps = jnp.einsum("qi,ixy->qxy", to_points, coarse, preferred_element_type=jnp.float32)
    heat = (
        capacity[:, None, None] * temps + latent[:, None, None] * jax.nn.sigmoid(2.0 * temps)
    ).astype(jnp.bfloat16)
    enthalpy = jnp.einsum("iq,qxy->ixy", from_points, heat, preferred_element_type=jnp.float32)
    return (mass_rows[None] * enthalpy + mixed).astype(jnp.bfloat16)


def body(field, kappa, mass, kl_modes, to_points, from_points, capacity, latent):
    coarse = field.astype(jnp.bfloat16)
    owned = coarse.shape[0]
    width = coarse.shape[2]
    groups = lax.axis_size("mode")
    terms = kappa.shape[0]
    kap_rows = lax.all_gather(kappa, "mode", axis=1, tiled=True)
    stacked = jnp.concatenate([coarse, kap_rows], 0)
    padded = extended(stacked, (("mesh", 1),), 1)
    images = conduct(padded[:owned], padded[owned:])
    joined = jnp.concatenate([coarse[None], images], 0)
    joined = joined.reshape((terms + 1) * owned, coarse.shape[1], width)
    moved = lax.all_to_all(joined, "mode", split_axis=1, concat_axis=0, tiled=True)
    node_rows = moved.shape[1]
    moved = moved.reshape(groups, terms + 1, owned, node_rows, width)
    moved = jnp.transpose(moved, (1, 0, 2, 3, 4)).reshape(
        terms + 1, groups * owned, node_rows, width
    )
    node_coarse = moved[0]
    node_images = moved[1:]
    result = finish(
        node_coarse, node_images, mass, kl_modes, to_points, from_points, capacity, latent
    )
    return lax.all_to_all(result, "mode", split_axis=0, concat_axis=1, tiled=True)


def solution(mesh):
    in_specs = (
        P("mode", "mesh", None),
        P(None, ("mesh", "mode"), None),
        P(("mesh", "mode"), None),
        P(),
        P(),
        P(),
        P(),
        P(),
    )
    out_specs = P("mode", "mesh", None)
    return jax.shard_map(body, mesh=mesh, in_specs=in_specs, out_specs=out_specs, check_vma=False)
```

profile of v0, /device:TPU:1, one launch (start us, length us, event | category | flops | bytes accessed | tf_op | source)
XLA Modules:
  0.0 1315.9 jit_solution(11272950333644281777)
XLA Ops:
  0.0 0.0 copy-start
  0.0 0.0 slice-start.2
  0.0 0.0 copy-start.2
  0.0 16.5 %copy.54 = bf16[32,128,1024]{2,0,1:T(8,128)(2,1)S(1)} copy(f32[32,128,1024]{2,1,0:T(8,128)} %param.8) | data formatting | bytes 25165824 | tf_op args[0]
  16.6 0.0 copy-done.2
  16.6 0.0 copy-start.1
  16.6 28.1 %all_gather.3 = bf16[3,128,1024]{2,1,0:T(8,128)(2,1)S(1)} all-gather(bf16[3,16,1024]{2,1,0:T(8,128)(2,1)S(1)} %copy-done.2), channel_id=1, replica_groups=mesh['mesh'=4,'mode'=8] {'mode'}, dimensions={1}, use_global_device_ids=true | all-gather | bytes 884736 | tf_op jit(solution)/shard_map/all_gather | solution.py:55
  44.6 0.7 copy.32
  45.3 0.0 slice-start.3
  45.4 9.1 collective-permute-start
  54.5 2.1 collective-permute-start.1
  56.7 0.0 slice-done
  56.7 0.0 slice-done.1
  56.7 0.0 slice-done.2
  56.7 0.0 slice-done.3
  56.7 11.4 copy.56
  68.1 0.0 collective-permute-done
  68.1 0.0 collective-permute-done.1
  68.1 0.0 copy-done.1
  68.1 12.0 fusion.11
  80.1 51.1 %fusion.6 = (f32[32,128,1024]{2,0,1:T(8,128)}, f32[32,128,1024]{2,0,1:T(8,128)}, f32[32,128,1024]{2,0,1:T(8,128)}, f32[32,128,1024]{2,0,1:T(8,128)}) fusion(f32[1,32,130,1026]{3,1,2,0:T(8,128)} %fusion.11), kind=kLoop, calls=%fused_computation.15 | loop fusion | flops 16777216 | bytes 150994944 | tf_op jit(solution)/shard_map/mul | solution.py:35
  131.2 2.9 fusion.38
  134.1 0.0 slice-start.6
  134.1 0.0 slice-start.7
  134.1 4.5 fusion.36
  138.6 0.0 slice-done.4
  138.6 0.0 slice-done.5
  138.7 0.0 slice-done.6
  138.7 0.0 slice-done.7
  138.7 46.6 %add_convert_fusion = bf16[3,32,128,1024]{3,1,0,2:T(8,128)(2,1)} fusion(f32[32,128,1024]{2,0,1:T(8,128)} %get-tuple-element.8, f32[3,128,1024]{2,0,1:T(4,128)S(1)} %get-tuple-element.14, f32[32,128,1024]{2,0,1:T(8,128)} %get-tuple-element.6, f32[3,128,1024]{2,0,1:T(4,128)S(1)} %get-tuple-element.12, f32[32,128,1024]{2,0,1:T(8,128)} %get-tuple-element.7, ...), kind=kLoop, calls=%fused_computation | loop fusion | flops 100663296 | bytes 98566144 | tf_op jit(solution)/shard_map/convert_element_type | solution.py:36
  185.3 23.1 %pad_maximum_fusion = bf16[4,32,128,1024]{3,1,0,2:T(8,128)(2,1)} fusion(bf16[3,32,128,1024]{3,1,0,2:T(8,128)(2,1)} %add_convert_fusion, bf16[1,32,128,1024]{3,1,0,2:T(8,128)(2,1)} %bitcast.79), kind=kLoop, calls=%fused_computation.1 | loop fusion | flops 16777216 | bytes 67108864 | tf_op jit(solution)/shard_map/concatenate | solution.py:59
  208.4 733.1 %all_to_all.33 = bf16[128,128,1024]{2,0,1:T(8,128)(2,1)} all-to-all(bf16[128,128,1024]{2,0,1:T(8,128)(2,1)} %bitcast.72), channel_id=1, replica_groups=mesh['mesh'=4,'mode'=8] {'mode'}, dimensions={1} | all-to-all | bytes 67108864 | tf_op jit(solution)/shard_map/all_to_all | solution.py:61
  941.5 30.8 %copy.35 = bf16[8,128,16,1024]{3,2,1,0:T(8,128)(2,1)} copy(bf16[8,128,16,1024]{3,1,2,0:T(8,128)(2,1)} %bitcast.73) | data formatting | bytes 67108864 | tf_op jit(solution)/shard_map/all_to_all | solution.py:61
  972.3 21.4 %slice.80 = bf16[3,8,32,16,1024]{4,3,2,0,1:T(8,128)(2,1)} slice(bf16[4,8,32,16,1024]{4,3,2,0,1:T(8,128)(2,1)} %bitcast.70), slice={[1:4], [0:8], [0:32], [0:16], [0:1024]} | slice | bytes 50331648 | tf_op jit(solution)/shard_map/slice | solution.py:68
  993.7 8.7 slice.79
  1002.4 21.3 %copy.37 = bf16[3,8,32,16,1024]{4,3,2,1,0:T(8,128)(2,1)} copy(bf16[3,8,32,16,1024]{4,3,2,0,1:T(8,128)(2,1)} %slice.80) | data formatting | bytes 50331648 | tf_op jit(solution)/shard_map/slice | solution.py:68
  1023.7 0.0 copy-done
  1023.7 0.0 copy-start.5
  1023.8 0.0 copy-start.6
  1023.8 0.0 copy-start.7
  1023.8 59.9 %fusion = f32[16,1024,256,1]{2,1,3,0:T(8,128)} fusion(bf16[3,256,16,1024]{3,2,1,0:T(8,128)(2,1)} %bitcast.80, bf16[3,256,256]{2,1,0:T(8,128)(2,1)S(1)} %copy-done), kind=kOutput, calls=%fused_computation.5 | convolution fusion | flops 6442450944 | bytes 42336256 | tf_op jit(solution)/shard_map/kij,kjxy->ixy/dot_general | solution.py:40
  1083.7 0.0 copy-done.3
  1083.7 0.0 copy-done.4
  1083.7 0.0 copy-done.5
  1083.8 22.9 %fusion.23 = bf16[256,16,1024]{0,2,1:T(8,128)(2,1)} fusion(f32[16,1024,256,1]{2,1,3,0:T(8,128)} %fusion, f32[512]{0:T(512)S(1)} %copy-done.6, f32[512]{0:T(512)S(1)} %copy-done.7, bf16[256,16,1024]{2,1,0:T(8,128)(2,1)} %bitcast.81, f32[16,1024]{1,0:T(8,128)S(1)} %copy-done.5, bf16[256,512]{1,0:T(8,128)(2,1)S(1)} %copy-done.3, bf16[512,256]{1,0:T(8,128)(2,1)S(1)} %copy-done.4), kind=kOutput, calls=%fused_computation.30 | convolution fusion | flops 8669626368 | bytes 34148352 | tf_op jit(solution)/shard_map/iq,qxy->ixy/dot_general | solution.py:45
  1106.6 12.2 copy.39
  1118.9 187.9 %all_to_all.34 = bf16[256,16,1024]{2,1,0:T(8,128)(2,1)} all-to-all(bf16[256,16,1024]{2,1,0:T(8,128)(2,1)} %copy.39), channel_id=1, replica_groups=mesh['mesh'=4,'mode'=8] {'mode'}, dimensions={0} | all-to-all | bytes 16777216 | tf_op jit(solution)/shard_map/all_to_all | solution.py:72
  1306.8 8.7 copy.40
  (11 shorter events, 0.0 us)
Async XLA Ops:
  0.0 1023.7 %copy-start = (bf16[3,256,256]{2,1,0:T(8,128)(2,1)S(1)}, bf16[3,256,256]{2,1,0:T(8,128)(2,1)}, u32[]{:S(2)}) copy-start(bf16[3,256,256]{2,1,0:T(8,128)(2,1)} %param.11) | copy-start | bytes 1179652
  0.0 56.6 %slice-start = ((s8[16777216]{0:T(1024)(128)(4,1)}), s8[4194304]{0:T(1024)(128)(4,1)S(1)}, s32[]{:S(2)}) async-start(s8[16777216]{0:T(1024)(128)(4,1)} %bitcast.74), calls=%async_computation.2 | async-start | bytes 8388608
  0.0 56.7 %slice-start.1 = ((s8[16777216]{0:T(1024)(128)(4,1)}), s8[4194304]{0:T(1024)(128)(4,1)S(1)}, s32[]{:S(2)}) async-start(s8[16777216]{0:T(1024)(128)(4,1)} %bitcast.74), calls=%async_computation.3 | async-start | bytes 8388608
  0.0 56.7 %slice-start.2 = ((s8[16777216]{0:T(1024)(128)(4,1)}), s8[4194304]{0:T(1024)(128)(4,1)S(1)}, s32[]{:S(2)}) async-start(s8[16777216]{0:T(1024)(128)(4,1)} %bitcast.74), calls=%async_computation.4 | async-start | bytes 8388608
  0.0 16.6 %copy-start.2 = (bf16[3,16,1024]{2,1,0:T(8,128)(2,1)S(1)}, bf16[3,16,1024]{2,1,0:T(8,128)(2,1)}, u32[]{:S(2)}) copy-start(bf16[3,16,1024]{2,1,0:T(8,128)(2,1)} %param.9) | copy-start | bytes 294916
  16.6 51.5 %copy-start.1 = (bf16[32,128,1024]{2,0,1:T(8,128)(2,1)}, bf16[32,128,1024]{2,0,1:T(8,128)(2,1)S(1)}, u32[]{:S(2)}) copy-start(bf16[32,128,1024]{2,0,1:T(8,128)(2,1)S(1)} %copy.54) | copy-start | bytes 25165828
  45.3 11.4 slice-start.3
  45.4 22.8 %collective-permute-start = (bf16[35,1,1024]{2,0,1:T(8,128)(2,1)S(1)}, bf16[35,1,1024]{2,0,1:T(8,128)(2,1)S(1)}, u32[]{:S(2)}, u32[]{:S(2)}) collective-permute-start(bf16[35,1,1024]{2,0,1:T(8,128)(2,1)S(1)} %get-tuple-element.9), channel_id=1, source_target_pairs={{0,8},{8,16},{16,24},{1,9},{9,17},{17,25},{2,10},{10,18},{18,26},{... | collective-permute-start | bytes 215048 | tf_op jit(solution)/shard_map/ppermute | solution.py:15
  54.5 13.6 %collective-permute-start.1 = (bf16[35,1,1024]{2,0,1:T(8,128)(2,1)S(1)}, bf16[35,1,1024]{2,0,1:T(8,128)(2,1)S(1)}, u32[]{:S(2)}, u32[]{:S(2)}) collective-permute-start(bf16[35,1,1024]{2,0,1:T(8,128)(2,1)S(1)} %get-tuple-element.10), channel_id=1, source_target_pairs={{8,0},{16,8},{24,16},{9,1},{17,9},{25,17},{10,2},{18,10},{26,18},{... | collective-permute-start | bytes 215048 | tf_op jit(solution)/shard_map/ppermute | solution.py:17
  131.2 7.5 slice-start.4
  131.2 7.5 slice-start.5
  134.1 4.6 slice-start.6
  134.1 4.6 slice-start.7
  1023.7 60.0 %copy-start.3 = (bf16[256,512]{1,0:T(8,128)(2,1)S(1)}, bf16[256,512]{1,0:T(8,128)(2,1)}, u32[]{:S(2)}) copy-start(bf16[256,512]{1,0:T(8,128)(2,1)} %param.13) | copy-start | bytes 786436
  1023.7 60.0 %copy-start.4 = (bf16[512,256]{1,0:T(8,128)(2,1)S(1)}, bf16[512,256]{1,0:T(8,128)(2,1)}, u32[]{:S(2)}) copy-start(bf16[512,256]{1,0:T(8,128)(2,1)} %param.12) | copy-start | bytes 786436
  1023.7 60.0 %copy-start.5 = (f32[16,1024]{1,0:T(8,128)S(1)}, f32[16,1024]{1,0:T(8,128)}, u32[]{:S(2)}) copy-start(f32[16,1024]{1,0:T(8,128)} %param.10) | copy-start | bytes 196612
  1023.8 60.0 %copy-start.6 = (f32[512]{0:T(512)S(1)}, f32[512]{0:T(512)}, u32[]{:S(2)}) copy-start(f32[512]{0:T(512)} %param.15) | copy-start | bytes 6148
  1023.8 60.0 %copy-start.7 = (f32[512]{0:T(512)S(1)}, f32[512]{0:T(512)}, u32[]{:S(2)}) copy-start(f32[512]{0:T(512)} %param.14) | copy-start | bytes 6148
where the time goes:
time: 1320 us
  blocking collectives  949 us (72%)
  other arithmetic  140 us (11%)
  local copies, waits for them, and re-layouts  132 us (10%)
  matrix products  82.8 us (6%)
    all_to_all x1, blocking collectives, body(): lax.all_to_all(joined, 'mode', split_axis=1, concat_axis=0, tiled=True)  733 us
    all_to_all x1, blocking collectives, body(): lax.all_to_all(result, 'mode', split_axis=0, concat_axis=1, tiled=True)  188 us
    dot_general x1, matrix products, finish(): jnp.einsum('kij,kjxy->ixy', kl_modes, images, preferred_element_type=jnp....  59.9 us
    mul x2, other arithmetic, conduct(): total = total + 0.5 * (kcentre + kother) * (centre - other)  55.6 us
    convert_element_type x1, other arithmetic, conduct(): return total.astype(jnp.bfloat16)  46.6 us
    slice x2, local copies, waits for them, and re-layouts, body(): node_images = moved[1:]  42.7 us
    all_to_all x1, local copies, waits for them, and re-layouts, body(): lax.all_to_all(joined, 'mode', split_axis=1, concat_axis=0, tiled=True)  30.8 us
    all_gather x1, blocking collectives, body(): kap_rows = lax.all_gather(kappa, 'mode', axis=1, tiled=True)  28.1 us
  transfers between devices with their start and end apart: 2, of which 0 were waited for; matrix products, arithmetic and copies ran while one was open for 1% of the time, Pallas kernels for 0%

commit v1 on v0

--- a/solution.py
+++ b/solution.py
@@ -2,6 +2,29 @@
 import jax.numpy as jnp
 from jax import lax
 from jax.sharding import PartitionSpec as P
+
+
+def in_blocks(x, dim, count):
+    shape = x.shape
+    blocks = x.reshape(*shape[:dim], count, shape[dim] // count, *shape[dim + 1 :])
+    return jnp.moveaxis(blocks, dim, 0)
+
+
+def joined_along(pieces, dim):
+    dims = list(pieces.shape[1:])
+    dims[dim] *= pieces.shape[0]
+    return jnp.moveaxis(pieces, 0, dim).reshape(dims)
+
+
+def exchange_directly(x, axis, split_dim, concat_dim):
+    size, index = (lax.axis_size(axis), lax.axis_index(axis))
+    pieces = in_blocks(x, split_dim, size)
+    gathered = [pieces[index]]
+    for step in range(1, size):
+        sent = pieces[(index + step) % size]
+        gathered.append(lax.ppermute(sent, axis, [(i, (i + step) % size) for i in range(size)]))
+    pieces = jnp.stack(gathered)[(index - jnp.arange(size)) % size]
+    return joined_along(pieces, concat_dim)
 
 
 def extended(cells, sides, width):
@@ -58,7 +81,7 @@
     images = conduct(padded[:owned], padded[owned:])
     joined = jnp.concatenate([coarse[None], images], 0)
     joined = joined.reshape((terms + 1) * owned, coarse.shape[1], width)
-    moved = lax.all_to_all(joined, "mode", split_axis=1, concat_axis=0, tiled=True)
+    moved = exchange_directly(joined, "mode", 1, 0)
     node_rows = moved.shape[1]
     moved = moved.reshape(groups, terms + 1, owned, node_rows, width)
     moved = jnp.transpose(moved, (1, 0, 2, 3, 4)).reshape(

time: 1320 us -> 1500 us (1.14)
  blocking collectives: 949 us -> 409 us
  waiting for transfers between devices: 0.01 us -> 408 us
  local copies, waits for them, and re-layouts: 132 us -> 313 us
  starting transfers between devices: 11.3 us -> 109 us
  matrix products: 82.8 us -> 101 us
    all_to_all x1 -> x0, blocking collectives: 733 us -> none  [body(): lax.all_to_all(joined, 'mode', split_axis=1, concat_axis=0, tiled=True)]
    ppermute x0 -> x7, waiting for transfers between devices: none -> 408 us  [exchange_directly(): lax.ppermute(sent, axis, [(i, (i + step) % size) for i in range(size)])]
    all_to_all x1, blocking collectives: 188 us -> 381 us  [body(): lax.all_to_all(result, 'mode', split_axis=0, concat_axis=1, tiled=True)]
    ppermute x0 -> x7, starting transfers between devices: none -> 97.6 us  [exchange_directly(): lax.ppermute(sent, axis, [(i, (i + step) % size) for i in range(size)])]
    mul x0 -> x8, local copies, waits for them, and re-layouts: none -> 82.9 us  [conduct(): total = total + 0.5 * (kcentre + kother) * (centre - other)]
    gather x0 -> x5, local copies, waits for them, and re-layouts: none -> 56.5 us  [exchange_directly(): pieces = jnp.stack(gathered)[(index - jnp.arange(size)) % size]]
    unnamed x34 -> x57, local copies, waits for them, and re-layouts: 28 us -> 63.4 us
    all_to_all x1 -> x0, local copies, waits for them, and re-layouts: 30.8 us -> none  [body(): lax.all_to_all(joined, 'mode', split_axis=1, concat_axis=0, tiled=True)]
  transfers between devices with their start and end apart: 2 -> 9, of which waited for: 0 -> 4; matrix products, arithmetic and copies ran while one was open for 1% -> 4% of each run, Pallas kernels for 0% -> 0%
where the time goes in v1:
time: 1500 us; the launch traced here: 1490 us
  blocking collectives  409 us (27%)
  waiting for transfers between devices  408 us (27%)
  local copies, waits for them, and re-layouts  313 us (21%)
  other arithmetic  150 us (10%)
  starting transfers between devices  109 us (7%)
  matrix products  101 us (7%)
    ppermute x7, waiting for transfers between devices, exchange_directly(): lax.ppermute(sent, axis, [(i, (i + step) % size) for i in range(size)])  408 us
    all_to_all x1, blocking collectives, body(): lax.all_to_all(result, 'mode', split_axis=0, concat_axis=1, tiled=True)  381 us
    ppermute x7, starting transfers between devices, exchange_directly(): lax.ppermute(sent, axis, [(i, (i + step) % size) for i in range(size)])  97.6 us
    mul x8, local copies, waits for them, and re-layouts, conduct(): total = total + 0.5 * (kcentre + kother) * (centre - other)  82.9 us
    dot_general x1, matrix products, finish(): jnp.einsum('kij,kjxy->ixy', kl_modes, images, preferred_element_type=jnp....  77.9 us
    unnamed x57, local copies, waits for them, and re-layouts  63.4 us
    gather x5, local copies, waits for them, and re-layouts, exchange_directly(): pieces = jnp.stack(gathered)[(index - jnp.arange(size)) % size]  56.5 us
    mul x2, other arithmetic, conduct(): total = total + 0.5 * (kcentre + kother) * (centre - other)  56.1 us
  transfers between devices with their start and end apart: 9, of which 4 were waited for; matrix products, arithmetic and copies ran while one was open for 4% of the time, Pallas kernels for 0%

profile of v1, /device:TPU:1, one launch (start us, length us, event | category | flops | bytes accessed | tf_op | source)
XLA Modules:
  0.0 1491.5 jit_solution(10087968989301413361)
XLA Ops:
  0.0 28.4 %all_gather.3 = bf16[3,128,1024]{2,1,0:T(8,128)(2,1)S(1)} all-gather(bf16[3,16,1024]{2,1,0:T(8,128)(2,1)} %param.9), channel_id=1, replica_groups=mesh['mesh'=4,'mode'=8] {'mode'}, dimensions={1}, use_global_device_ids=true | all-gather | bytes 884736 | tf_op jit(solution)/shard_map/all_gather | solution.py:78
  29.1 16.5 %copy.64 = bf16[32,128,1024]{2,0,1:T(8,128)(2,1)S(1)} copy(f32[32,128,1024]{2,1,0:T(8,128)} %param.8) | data formatting | bytes 25165824 | tf_op args[0]
  45.7 8.0 collective-permute-start.1
  53.7 3.7 collective-permute-start
  57.4 11.4 copy.66
  68.8 11.4 copy.46
  80.2 14.2 fusion.11
  94.5 51.6 %fusion.6 = (f32[32,128,1024]{2,0,1:T(8,128)}, f32[32,128,1024]{2,0,1:T(8,128)}, f32[32,128,1024]{2,0,1:T(8,128)}, f32[32,128,1024]{2,0,1:T(8,128)}) fusion(f32[1,32,130,1026]{3,1,2,0:T(8,128)} %fusion.11), kind=kLoop, calls=%fused_computation.19 | loop fusion | flops 16777216 | bytes 150994944 | tf_op jit(solution)/shard_map/mul | solution.py:58
  146.1 17.7 %copy.45 = f32[32,128,1024]{2,1,0:T(8,128)} copy(f32[32,128,1024]{2,0,1:T(8,128)} %get-tuple-element.17) | data formatting | bytes 33554432 | tf_op jit(solution)/shard_map/mul | solution.py:58
  163.7 2.8 fusion.38
  166.6 4.5 fusion.36
  172.1 21.0 %copy.43 = f32[32,128,1024]{2,1,0:T(8,128)} copy(f32[32,128,1024]{2,0,1:T(8,128)} %get-tuple-element.15) | data formatting | bytes 33554432 | tf_op jit(solution)/shard_map/mul | solution.py:58
  193.0 2.1 copy.42
  195.2 19.1 %copy.41 = f32[32,128,1024]{2,1,0:T(8,128)} copy(f32[32,128,1024]{2,0,1:T(8,128)S(1)} %bitcast.104) | data formatting | bytes 33554432 | tf_op jit(solution)/shard_map/mul | solution.py:58
  214.2 2.0 copy.40
  216.3 19.3 %copy.39 = f32[32,128,1024]{2,1,0:T(8,128)} copy(f32[32,128,1024]{2,0,1:T(8,128)S(1)} %bitcast.102) | data formatting | bytes 33554432 | tf_op jit(solution)/shard_map/mul | solution.py:58
  236.6 31.3 %add_convert_fusion = bf16[3,32,128,1024]{3,2,1,0:T(8,128)(2,1)} fusion(f32[32,128,1024]{2,1,0:T(8,128)S(1)} %bitcast.108, f32[3,128,1024]{2,1,0:T(8,128)S(1)} %copy.44, f32[32,128,1024]{2,1,0:T(8,128)} %copy.43, f32[3,128,1024]{2,1,0:T(8,128)S(1)} %copy-done.2, f32[32,128,1024]{2,1,0:T(8,128)} %copy.41, f32[3,128,1024]{2,1,0:T(8,128)} %copy.40, ...), kind=kLoop, calls=%fused_computation.3 | loop fusion | flops 100663296 | bytes 98566144 | tf_op jit(solution)/shard_map/convert_element_type | solution.py:59
  267.9 23.1 %pad_maximum_fusion = bf16[4,32,128,1024]{3,2,1,0:T(8,128)(2,1)} fusion(bf16[3,32,128,1024]{3,2,1,0:T(8,128)(2,1)} %add_convert_fusion, bf16[1,32,128,1024]{3,2,1,0:T(8,128)(2,1)} %copy.46), kind=kLoop, calls=%fused_computation.4 | loop fusion | flops 16777216 | bytes 67108864 | tf_op jit(solution)/shard_map/concatenate | solution.py:82
  291.0 20.6 %dynamic-slice_bitcast_fusion = (bf16[128,16,1024]{2,1,0:T(8,128)(2,1)}, bf16[128,16,1024]{2,1,0:T(8,128)(2,1)}, bf16[128,16,1024]{2,1,0:T(8,128)(2,1)}, bf16[12...) fusion(bf16[128,8,16,1024]{3,2,1,0:T(8,128)(2,1)} %bitcast.99, ...), kind=kLoop, calls=%fused_computation.43 | loop fusion | bytes 58720284 | tf_op jit(solution)/shard_map/squeeze | solution.py:24
  311.6 1.3 collective-permute-start.2
  313.8 2.5 collective-permute-start.5
  316.2 3.2 collective-permute-start.6
  319.5 87.7 %collective-permute-done.2 = bf16[128,16,1024]{2,1,0:T(8,128)(2,1)} collective-permute-done((bf16[128,16,1024]{2,1,0:T(8,128)(2,1)}, bf16[128,16,1024]{2,1,0:T(8,128)(2,1)}, u32[]{:S(2)}, u32[]{:S(2)}) %collective-permute-start.2) | collective-permute-done | bytes 4194336 | tf_op jit(solution)/shard_map/ppermute | solution.py:25
  407.7 89.8 %collective-permute-start.8 = (bf16[128,16,1024]{2,1,0:T(8,128)(2,1)}, bf16[128,16,1024]{2,1,0:T(8,128)(2,1)}, u32[]{:S(2)}, u32[]{:S(2)}) collective-permute-start(bf16[128,16,1024]{2,1,0:T(8,128)(2,1)} %get-tuple-element.7), channel_id=1, source_target_pairs={{0,7},{1,0},{2,1},{3,2},{4,3},{5,4},{6,5},{7,6},{8,15},{9,8},{10,9... | collective-permute-start | bytes 12582920 | tf_op jit(solution)/shard_map/ppermute | solution.py:25
  497.5 5.1 bitcast_dynamic-update-slice_fusion.7
  502.6 5.0 bitcast_dynamic-update-slice_fusion.6
  507.6 5.0 bitcast_dynamic-update-slice_fusion.5
  512.7 253.9 %collective-permute-done.4 = bf16[128,16,1024]{2,1,0:T(8,128)(2,1)} collective-permute-done((bf16[128,16,1024]{2,1,0:T(8,128)(2,1)}, bf16[128,16,1024]{2,1,0:T(8,128)(2,1)}, u32[]{:S(2)}, u32[]{:S(2)}) %collective-permute-start.4) | collective-permute-done | bytes 4194336 | tf_op jit(solution)/shard_map/ppermute | solution.py:25
  766.5 5.0 bitcast_dynamic-update-slice_fusion.4
  771.5 5.1 bitcast_dynamic-update-slice_fusion.3
  776.7 5.0 bitcast_dynamic-update-slice_fusion.2
  781.7 5.0 bitcast_dynamic-update-slice_fusion.1
  786.7 66.1 %collective-permute-done.8 = bf16[128,16,1024]{2,1,0:T(8,128)(2,1)} collective-permute-done((bf16[128,16,1024]{2,1,0:T(8,128)(2,1)}, bf16[128,16,1024]{2,1,0:T(8,128)(2,1)}, u32[]{:S(2)}, u32[]{:S(2)}) %collective-permute-start.8) | collective-permute-done | bytes 4194336 | tf_op jit(solution)/shard_map/ppermute | solution.py:25
  852.8 5.0 bitcast_dynamic-update-slice_fusion
  857.8 7.3 mini-gather-slice.5
  865.1 18.3 %fusion.50 = (bf16[8,128,16,384]{3,2,1,0:T(8,128)(2,1)}, bf16[8,128,16,384]{3,2,1,0:T(8,128)(2,1)}) fusion(bf16[8,128,16,1024]{3,2,1,0:T(8,128)(2,1)} %bitcast_dynamic-update-slice_fusion), kind=kLoop, calls=%fused_computation.86 | loop fusion | bytes 50331648 | tf_op jit(solution)/shard_map/gather | solution.py:26
  883.4 8.1 gather_fusion.2
  891.5 11.4 gather_fusion.1
  902.9 11.4 gather_fusion
  914.3 22.8 %pad_maximum_fusion.1 = bf16[8,128,16,1024]{3,2,1,0:T(8,128)(2,1)} fusion(bf16[8,128,16,256]{3,2,1,0:T(8,128)(2,1)} %gather_fusion.2, bf16[8,128,16,384]{3,2,1,0:T(8,128)(2,1)} %gather_fusion.1, bf16[8,128,16,384]{3,2,1,0:T(8,128)(2,1)} %gather_fusion), kind=kLoop, calls=%fused_computation.5 | loop fusion | flops 100663296 | bytes 67108864
  937.1 21.3 %slice.86 = bf16[3,8,32,16,1024]{4,3,2,0,1:T(8,128)(2,1)} slice(bf16[4,8,32,16,1024]{4,3,2,0,1:T(8,128)(2,1)} %bitcast.97), slice={[1:4], [0:8], [0:32], [0:16], [0:1024]} | slice | bytes 50331648 | tf_op jit(solution)/shard_map/slice | solution.py:91
  958.4 8.7 slice.85
  967.1 21.4 %copy.48 = bf16[3,8,32,16,1024]{4,3,2,1,0:T(8,128)(2,1)} copy(bf16[3,8,32,16,1024]{4,3,2,0,1:T(8,128)(2,1)} %slice.86) | data formatting | bytes 50331648 | tf_op jit(solution)/shard_map/slice | solution.py:91
  988.5 77.9 %fusion = f32[16,1024,256,1]{2,1,3,0:T(8,128)} fusion(bf16[3,256,16,1024]{3,2,1,0:T(8,128)(2,1)} %bitcast.111, bf16[3,256,256]{2,1,0:T(8,128)(2,1)S(1)} %copy-done), kind=kOutput, calls=%fused_computation.9 | convolution fusion | flops 6442450944 | bytes 42336256 | tf_op jit(solution)/shard_map/kij,kjxy->ixy/dot_general | solution.py:63
  1066.4 22.8 %fusion.23 = bf16[256,16,1024]{0,2,1:T(8,128)(2,1)} fusion(f32[16,1024,256,1]{2,1,3,0:T(8,128)} %fusion, f32[512]{0:T(512)S(1)} %copy-done.6, f32[512]{0:T(512)S(1)} %copy-done.7, bf16[256,16,1024]{2,1,0:T(8,128)(2,1)} %bitcast.112, f32[16,1024]{1,0:T(8,128)S(1)} %copy-done.5, bf16[256,512]{1,0:T(8,128)(2,1)S(1)} %copy-done.3, ...), kind=kOutput, calls=%fused_computation.34 | convolution fusion | flops 8669626368 | bytes 34148352 | tf_op jit(solution)/shard_map/iq,qxy->ixy/dot_general | solution.py:68
  1089.2 12.2 copy.50
  1101.5 380.9 %all_to_all.18 = bf16[256,16,1024]{2,1,0:T(8,128)(2,1)} all-to-all(bf16[256,16,1024]{2,1,0:T(8,128)(2,1)} %copy.50), channel_id=1, replica_groups=mesh['mesh'=4,'mode'=8] {'mode'}, dimensions={0} | all-to-all | bytes 16777216 | tf_op jit(solution)/shard_map/all_to_all | solution.py:95
  1482.4 8.7 copy.51
  (67 shorter events, 4.0 us)
Async XLA Ops:
  0.0 988.4 %copy-start = (bf16[3,256,256]{2,1,0:T(8,128)(2,1)S(1)}, bf16[3,256,256]{2,1,0:T(8,128)(2,1)}, u32[]{:S(2)}) copy-start(bf16[3,256,256]{2,1,0:T(8,128)(2,1)} %param.11) | copy-start | bytes 1179652
  29.1 28.3 %slice-start.8 = ((s8[16777216]{0:T(1024)(128)(4,1)}), s8[4194304]{0:T(1024)(128)(4,1)S(1)}, s32[]{:S(2)}) async-start(s8[16777216]{0:T(1024)(128)(4,1)} %bitcast.105), calls=%async_computation.9 | async-start | bytes 8388608
  29.1 28.3 %slice-start.9 = ((s8[16777216]{0:T(1024)(128)(4,1)}), s8[4194304]{0:T(1024)(128)(4,1)S(1)}, s32[]{:S(2)}) async-start(s8[16777216]{0:T(1024)(128)(4,1)} %bitcast.105), calls=%async_computation.10 | async-start | bytes 8388608
  29.1 28.3 %slice-start.10 = ((s8[16777216]{0:T(1024)(128)(4,1)}), s8[4194304]{0:T(1024)(128)(4,1)S(1)}, s32[]{:S(2)}) async-start(s8[16777216]{0:T(1024)(128)(4,1)} %bitcast.105), calls=%async_computation.11 | async-start | bytes 8388608
  45.6 23.2 %copy-start.1 = (bf16[32,128,1024]{2,0,1:T(8,128)(2,1)}, bf16[32,128,1024]{2,0,1:T(8,128)(2,1)S(1)}, u32[]{:S(2)}) copy-start(bf16[32,128,1024]{2,0,1:T(8,128)(2,1)S(1)} %copy.64) | copy-start | bytes 25165828
  45.6 11.7 slice-start.11
  45.7 34.6 %collective-permute-start.1 = (bf16[35,1,1024]{2,0,1:T(8,128)(2,1)S(1)}, bf16[35,1,1024]{2,0,1:T(8,128)(2,1)S(1)}, u32[]{:S(2)}, u32[]{:S(2)}) collective-permute-start(bf16[35,1,1024]{2,0,1:T(8,128)(2,1)S(1)} %get-tuple-element.19), channel_id=1, source_target_pairs={{8,0},{16,8},{24,16},{9,1},{17,9},{25,17},{10,2},{18,10},{26,18},{... | collective-permute-start | bytes 215048 | tf_op jit(solution)/shard_map/ppermute | solution.py:40
  53.7 26.6 %collective-permute-start = (bf16[35,1,1024]{2,0,1:T(8,128)(2,1)S(1)}, bf16[35,1,1024]{2,0,1:T(8,128)(2,1)S(1)}, u32[]{:S(2)}, u32[]{:S(2)}) collective-permute-start(bf16[35,1,1024]{2,0,1:T(8,128)(2,1)S(1)} %get-tuple-element.18), channel_id=1, source_target_pairs={{0,8},{8,16},{16,24},{1,9},{9,17},{17,25},{2,10},{10,18},{18,26},{... | collective-permute-start | bytes 215048 | tf_op jit(solution)/shard_map/ppermute | solution.py:38
  172.0 23.1 %slice-start.4 = ((s8[16777216]{0:T(1024)(128)(4,1)}), s8[4194304]{0:T(1024)(128)(4,1)S(1)}, s32[]{:S(2)}) async-start(s8[16777216]{0:T(1024)(128)(4,1)} %bitcast.103), calls=%async_computation.5 | async-start | bytes 8388608
  172.1 23.1 %slice-start.5 = ((s8[16777216]{0:T(1024)(128)(4,1)}), s8[4194304]{0:T(1024)(128)(4,1)S(1)}, s32[]{:S(2)}) async-start(s8[16777216]{0:T(1024)(128)(4,1)} %bitcast.103), calls=%async_computation.6 | async-start | bytes 8388608
  172.1 23.0 %slice-start.6 = ((s8[16777216]{0:T(1024)(128)(4,1)}), s8[4194304]{0:T(1024)(128)(4,1)S(1)}, s32[]{:S(2)}) async-start(s8[16777216]{0:T(1024)(128)(4,1)} %bitcast.103), calls=%async_computation.7 | async-start | bytes 8388608
  172.1 23.0 %slice-start.7 = ((s8[16777216]{0:T(1024)(128)(4,1)}), s8[4194304]{0:T(1024)(128)(4,1)S(1)}, s32[]{:S(2)}) async-start(s8[16777216]{0:T(1024)(128)(4,1)} %bitcast.103), calls=%async_computation.8 | async-start | bytes 8388608
  195.1 21.2 %slice-start = ((s8[16777216]{0:T(1024)(128)(4,1)}), s8[4194304]{0:T(1024)(128)(4,1)S(1)}, s32[]{:S(2)}) async-start(s8[16777216]{0:T(1024)(128)(4,1)} %bitcast.101), calls=%async_computation.1 | async-start | bytes 8388608
  195.1 21.1 %slice-start.1 = ((s8[16777216]{0:T(1024)(128)(4,1)}), s8[4194304]{0:T(1024)(128)(4,1)S(1)}, s32[]{:S(2)}) async-start(s8[16777216]{0:T(1024)(128)(4,1)} %bitcast.101), calls=%async_computation.2 | async-start | bytes 8388608
  195.1 21.1 %slice-start.2 = ((s8[16777216]{0:T(1024)(128)(4,1)}), s8[4194304]{0:T(1024)(128)(4,1)S(1)}, s32[]{:S(2)}) async-start(s8[16777216]{0:T(1024)(128)(4,1)} %bitcast.101), calls=%async_computation.3 | async-start | bytes 8388608
  195.2 21.1 %slice-start.3 = ((s8[16777216]{0:T(1024)(128)(4,1)}), s8[4194304]{0:T(1024)(128)(4,1)S(1)}, s32[]{:S(2)}) async-start(s8[16777216]{0:T(1024)(128)(4,1)} %bitcast.101), calls=%async_computation.4 | async-start | bytes 8388608
  216.3 20.2 %slice-start.12 = ((s8[16777216]{0:T(1024)(128)(4,1)}), s8[4194304]{0:T(1024)(128)(4,1)S(1)}, s32[]{:S(2)}) async-start(s8[16777216]{0:T(1024)(128)(4,1)} %bitcast.107), calls=%async_computation.13 | async-start | bytes 8388608
  216.3 20.2 %slice-start.13 = ((s8[16777216]{0:T(1024)(128)(4,1)}), s8[4194304]{0:T(1024)(128)(4,1)S(1)}, s32[]{:S(2)}) async-start(s8[16777216]{0:T(1024)(128)(4,1)} %bitcast.107), calls=%async_computation.14 | async-start | bytes 8388608
  216.3 20.2 %slice-start.14 = ((s8[16777216]{0:T(1024)(128)(4,1)}), s8[4194304]{0:T(1024)(128)(4,1)S(1)}, s32[]{:S(2)}) async-start(s8[16777216]{0:T(1024)(128)(4,1)} %bitcast.107), calls=%async_computation.15 | async-start | bytes 8388608
  216.3 20.2 %slice-start.15 = ((s8[16777216]{0:T(1024)(128)(4,1)}), s8[4194304]{0:T(1024)(128)(4,1)S(1)}, s32[]{:S(2)}) async-start(s8[16777216]{0:T(1024)(128)(4,1)} %bitcast.107), calls=%async_computation.16 | async-start | bytes 8388608
  216.3 20.2 %copy-start.2 = (f32[3,128,1024]{2,1,0:T(8,128)S(1)}, f32[3,128,1024]{2,1,0:T(8,128)}, u32[]{:S(2)}) copy-start(f32[3,128,1024]{2,1,0:T(8,128)} %copy.42) | copy-start | bytes 4718596
  311.6 95.5 %collective-permute-start.2 = (bf16[128,16,1024]{2,1,0:T(8,128)(2,1)}, bf16[128,16,1024]{2,1,0:T(8,128)(2,1)}, u32[]{:S(2)}, u32[]{:S(2)}) collective-permute-start(bf16[128,16,1024]{2,1,0:T(8,128)(2,1)} %get-tuple-element.13), channel_id=1, source_target_pairs={{0,1},{1,2},{2,3},{3,4},{4,5},{5,6},{6,7},{7,0},{8,9},{9,10},{10,1... | collective-permute-start | bytes 12582920 | tf_op jit(solution)/shard_map/ppermute | solution.py:25
  312.9 94.7 %collective-permute-start.3 = (bf16[128,16,1024]{2,1,0:T(8,128)(2,1)}, bf16[128,16,1024]{2,1,0:T(8,128)(2,1)}, u32[]{:S(2)}, u32[]{:S(2)}) collective-permute-start(bf16[128,16,1024]{2,1,0:T(8,128)(2,1)} %get-tuple-element.12), channel_id=1, source_target_pairs={{0,2},{1,3},{2,4},{3,5},{4,6},{5,7},{6,0},{7,1},{8,10},{9,11},{10,... | collective-permute-start | bytes 12582920 | tf_op jit(solution)/shard_map/ppermute | solution.py:25
  312.9 453.6 %collective-permute-start.4 = (bf16[128,16,1024]{2,1,0:T(8,128)(2,1)}, bf16[128,16,1024]{2,1,0:T(8,128)(2,1)}, u32[]{:S(2)}, u32[]{:S(2)}) collective-permute-start(bf16[128,16,1024]{2,1,0:T(8,128)(2,1)} %get-tuple-element.11), channel_id=1, source_target_pairs={{0,3},{1,4},{2,5},{3,6},{4,7},{5,0},{6,1},{7,2},{8,11},{9,12},{10,... | collective-permute-start | bytes 12582920 | tf_op jit(solution)/shard_map/ppermute | solution.py:25
  313.8 457.8 %collective-permute-start.5 = (bf16[128,16,1024]{2,1,0:T(8,128)(2,1)}, bf16[128,16,1024]{2,1,0:T(8,128)(2,1)}, u32[]{:S(2)}, u32[]{:S(2)}) collective-permute-start(bf16[128,16,1024]{2,1,0:T(8,128)(2,1)} %get-tuple-element.10), channel_id=1, source_target_pairs={{0,4},{1,5},{2,6},{3,7},{4,0},{5,1},{6,2},{7,3},{8,12},{9,13},{10,... | collective-permute-start | bytes 12582920 | tf_op jit(solution)/shard_map/ppermute | solution.py:25
  316.2 460.4 %collective-permute-start.6 = (bf16[128,16,1024]{2,1,0:T(8,128)(2,1)}, bf16[128,16,1024]{2,1,0:T(8,128)(2,1)}, u32[]{:S(2)}, u32[]{:S(2)}) collective-permute-start(bf16[128,16,1024]{2,1,0:T(8,128)(2,1)} %get-tuple-element.9), channel_id=1, source_target_pairs={{0,5},{1,6},{2,7},{3,0},{4,1},{5,2},{6,3},{7,4},{8,13},{9,14},{10,... | collective-permute-start | bytes 12582920 | tf_op jit(solution)/shard_map/ppermute | solution.py:25
  407.2 374.5 %collective-permute-start.7 = (bf16[128,16,1024]{2,1,0:T(8,128)(2,1)}, bf16[128,16,1024]{2,1,0:T(8,128)(2,1)}, u32[]{:S(2)}, u32[]{:S(2)}) collective-permute-start(bf16[128,16,1024]{2,1,0:T(8,128)(2,1)} %get-tuple-element.8), channel_id=1, source_target_pairs={{0,6},{1,7},{2,0},{3,1},{4,2},{5,3},{6,4},{7,5},{8,14},{9,15},{10,... | collective-permute-start | bytes 12582920 | tf_op jit(solution)/shard_map/ppermute | solution.py:25
  407.7 445.1 %collective-permute-start.8 = (bf16[128,16,1024]{2,1,0:T(8,128)(2,1)}, bf16[128,16,1024]{2,1,0:T(8,128)(2,1)}, u32[]{:S(2)}, u32[]{:S(2)}) collective-permute-start(bf16[128,16,1024]{2,1,0:T(8,128)(2,1)} %get-tuple-element.7), channel_id=1, source_target_pairs={{0,7},{1,0},{2,1},{3,2},{4,3},{5,4},{6,5},{7,6},{8,15},{9,8},{10,9... | collective-permute-start | bytes 12582920 | tf_op jit(solution)/shard_map/ppermute | solution.py:25
  988.4 77.9 %copy-start.3 = (bf16[256,512]{1,0:T(8,128)(2,1)S(1)}, bf16[256,512]{1,0:T(8,128)(2,1)}, u32[]{:S(2)}) copy-start(bf16[256,512]{1,0:T(8,128)(2,1)} %param.13) | copy-start | bytes 786436
  988.4 77.9 %copy-start.4 = (bf16[512,256]{1,0:T(8,128)(2,1)S(1)}, bf16[512,256]{1,0:T(8,128)(2,1)}, u32[]{:S(2)}) copy-start(bf16[512,256]{1,0:T(8,128)(2,1)} %param.12) | copy-start | bytes 786436
  988.5 78.0 %copy-start.5 = (f32[16,1024]{1,0:T(8,128)S(1)}, f32[16,1024]{1,0:T(8,128)}, u32[]{:S(2)}) copy-start(f32[16,1024]{1,0:T(8,128)} %param.10) | copy-start | bytes 196612
  988.5 78.0 %copy-start.6 = (f32[512]{0:T(512)S(1)}, f32[512]{0:T(512)}, u32[]{:S(2)}) copy-start(f32[512]{0:T(512)} %param.15) | copy-start | bytes 6148
  988.5 77.9 %copy-start.7 = (f32[512]{0:T(512)S(1)}, f32[512]{0:T(512)}, u32[]{:S(2)}) copy-start(f32[512]{0:T(512)} %param.14) | copy-start | bytes 6148
